TPU v7x, 32 devices: a whole 2x2x4 slice. The times are simulated.
32 devices in a mesh: groups: 2 (over y), seq: 16 (over z, x, core).
Axes of the slice: x: 2, y: 2, z: 4, core: 2. Of those that a mesh axis runs over, the one named last changes fastest.
Arguments:
- queries: bfloat16 [8192, 2048], P(('groups', 'seq')), parts along dimension 0
- keys: bfloat16 [8192, 2048], P(('groups', 'seq')), parts along dimension 0
- values: bfloat16 [8192, 2048], P(('groups', 'seq')), parts along dimension 0, may hold values from -6 to 6
- grad_out: bfloat16 [8192, 2048], P(('groups', 'seq')), parts along dimension 0, may hold values from -15 to 15
- global_blocks: int32 [4], P('groups'), parts along dimension 0, may hold values from 0 to 63, as said below
- random_blocks: int32 [32, 64, 3], P('groups'), parts along dimension 0, may hold values from 0 to 63, as said below
Outputs:
- attended: bfloat16 [8192, 2048], P(('groups', 'seq')), parts along dimension 0
- grad_q: bfloat16 [8192, 2048], P(('groups', 'seq')), parts along dimension 0
- grad_k: bfloat16 [8192, 2048], P(('groups', 'seq')), parts along dimension 0
- grad_v: bfloat16 [8192, 2048], P(('groups', 'seq')), parts along dimension 0
There are 2 independent parts, one for each index of `groups`. A program takes and returns all parts, laid end to end along the dimension named above; each array names one. Nothing has to cross between parts.
Inputs may be any that keep to these rules, and one draw needn't show every extreme that they name: `global_blocks`: the 2 entries are distinct blocks. `random_blocks`: among the 192 entries for the query blocks of one index s of seq (blocks s * 4 to s * 4 + 3, all heads and slots), at most 12 name blocks of any one index of seq, and in every draw some index is named exactly 12 times by some index.
All inputs are finite; a program needn't handle non-finite values.
Results may differ from a plain program's by a relative error of at most 0.0057.
Values may be sent and summed in bfloat16 or wider, within the bound.
A program may use at most 192 MiB of HBM per device.

v0:
```python
import math

import jax
import jax.numpy as jnp
from jax import lax
from jax.sharding import PartitionSpec as P

HEADS = 16
HEAD_DIM = 128
BLOCK = 64
GLOBALS = 2
RANDOM = 3


MASKED = -1e30


def with_halo(shard, sides, width):
    for axis, dim in sides:
        peers, length = (lax.axis_size(axis), shard.shape[dim])
        up = [(i, (i + 1) % peers) for i in range(peers - 1)]
        down = [(j, i) for i, j in up]
        last = lax.slice_in_dim(shard, length - width, length, axis=dim)
        initial = lax.slice_in_dim(shard, 0, width, axis=dim)
        before = lax.ppermute(last, axis, up)
        after = lax.ppermute(initial, axis, down)
        shard = jnp.concatenate([before, shard, after], axis=dim)
    return shard


def from_root(value, axis, source):
    kept = jnp.where(lax.axis_index(axis) == source, value, 0).astype(value.dtype)
    return lax.psum(kept, axis)


def passed_along(value, axis, steps):
    count = lax.axis_size(axis)
    initial, last = (max(0, -steps), min(count, count - steps))
    return lax.ppermute(value, axis, [(source, source + steps) for source in range(initial, last)])


def on_device(queries, keys, values, grad_out, global_blocks, random_blocks):
    shards = lax.axis_size("seq")
    own_index = lax.axis_index("seq")
    local_count = queries.shape[0] // BLOCK
    total_blocks = local_count * shards
    score_scale = 1.0 / math.sqrt(HEAD_DIM)
    f32 = jnp.float32
    q_local = queries.reshape(local_count, BLOCK, HEADS, HEAD_DIM)
    d_local = grad_out.reshape(local_count, BLOCK, HEADS, HEAD_DIM)
    q_heads = jnp.transpose(q_local, (0, 2, 1, 3))
    d_heads = jnp.transpose(d_local, (0, 2, 1, 3))
    key_value = jnp.stack([keys, values], 0)
    kv_blocks = key_value.reshape(2, local_count, BLOCK, HEADS, HEAD_DIM)
    my_rows = lax.dynamic_slice_in_dim(random_blocks, own_index * local_count, local_count, 1)
    wanted = my_rows.reshape(-1)
    requests = wanted.shape[0]
    capacity = (requests + shards - 1) // shards
    owner_of = wanted // local_count
    peer_ids = jnp.arange(shards, dtype=jnp.int32)
    owner_hits = (owner_of[:, None] == peer_ids[None, :]).astype(jnp.int32)
    slot_rank = jnp.sum((jnp.cumsum(owner_hits, 0) - owner_hits) * owner_hits, 1)
    item_ids = jnp.arange(requests, dtype=jnp.int32)
    item_head = item_ids // (local_count * RANDOM)
    requested = jnp.transpose(
        random_blocks.reshape(HEADS, shards, local_count, RANDOM), (1, 0, 2, 3)
    )
    requested = requested.reshape(shards, requests)
    served = (requested // local_count == own_index).astype(jnp.int32)
    serve_rank = jnp.cumsum(served, 1) - served
    slot_ids = jnp.arange(capacity, dtype=jnp.int32)
    chosen = served[:, :, None] * (serve_rank[:, :, None] == slot_ids[None, None, :]).astype(
        jnp.int32
    )
    filled = jnp.sum(chosen, 1)
    code_head = jnp.sum(chosen * item_head[None, :, None], 1)
    code_block = jnp.sum(chosen * (requested % local_count)[:, :, None], 1)
    outgoing = kv_blocks[:, code_block, :, code_head, :]
    outgoing = jnp.where(filled[:, :, None, None, None] > 0, outgoing, jnp.zeros_like(outgoing))
    fetched = lax.all_to_all(outgoing, "seq", split_axis=0, concat_axis=0, tiled=True)
    arrived = fetched[owner_of, slot_rank].reshape(HEADS, local_count, RANDOM, 2, BLOCK, HEAD_DIM)
    rand_set = jnp.transpose(arrived, (3, 1, 0, 2, 4, 5)).reshape(
        2, local_count, HEADS, RANDOM * BLOCK, HEAD_DIM
    )
    padded = with_halo(key_value, (("seq", 1),), BLOCK)
    beside_all = jnp.transpose(
        padded.reshape(2, local_count + 2, BLOCK, HEADS, HEAD_DIM), (0, 1, 3, 2, 4)
    )
    near_set = jnp.stack([beside_all[:, offset : offset + local_count] for offset in range(3)], 3)
    near_set = near_set.reshape(2, local_count, HEADS, 3 * BLOCK, HEAD_DIM)
    global_list = []
    for global_slot in range(GLOBALS):
        target = global_blocks[global_slot]
        block_rows = lax.dynamic_index_in_dim(kv_blocks, target % local_count, 1, keepdims=False)
        global_list.append(from_root(block_rows, "seq", target // local_count))
    global_pair = jnp.stack(global_list, 1)
    glob_set = jnp.transpose(global_pair, (0, 3, 1, 2, 4)).reshape(
        2, HEADS, GLOBALS * BLOCK, HEAD_DIM
    )
    glob_set = jnp.broadcast_to(
        glob_set[:, None], (2, local_count, HEADS, GLOBALS * BLOCK, HEAD_DIM)
    )
    key_set = jnp.concatenate([near_set, glob_set, rand_set], 3)
    n_near = 3 * BLOCK
    n_glob = GLOBALS * BLOCK
    n_keys = key_set.shape[3]
    near_ids = (
        own_index * local_count
        + jnp.arange(local_count, dtype=jnp.int32)[:, None]
        + jnp.arange(3, dtype=jnp.int32)[None, :]
        - 1
    )
    inside = (near_ids >= 0) & (near_ids < total_blocks)
    column_valid = jnp.concatenate(
        [jnp.repeat(inside, BLOCK, 1), jnp.ones((local_count, n_keys - n_near), bool)], 1
    )
    scores = (
        jnp.einsum("jhqe,jhke->jhqk", q_heads, key_set[0], preferred_element_type=f32) * score_scale
    )
    scores = jnp.where(column_valid[:, None, None, :], scores, MASKED)
    row_max = jnp.max(scores, -1, keepdims=True)
    exponent = jnp.exp(scores - row_max)
    row_total = jnp.sum(exponent, -1, keepdims=True)
    probs = exponent / row_total
    probs_b = probs.astype(jnp.bfloat16)
    attended = jnp.einsum("jhqk,jhke->jhqe", probs_b, key_set[1], preferred_element_type=f32)
    grad_probs = jnp.einsum("jhqe,jhke->jhqk", d_heads, key_set[1], preferred_element_type=f32)
    delta = jnp.sum(probs * grad_probs, -1, keepdims=True)
    grad_scores = (probs * (grad_probs - delta)).astype(jnp.bfloat16)
    grad_q = score_scale * jnp.einsum(
        "jhqk,jhke->jhqe", grad_scores, key_set[0], preferred_element_type=f32
    )
    near_k = score_scale * jnp.einsum(
        "jhqk,jhqe->jhke", grad_scores[..., :n_near], q_heads, preferred_element_type=f32
    )
    near_v = jnp.einsum(
        "jhqk,jhqe->jhke", probs_b[..., :n_near], d_heads, preferred_element_type=f32
    )
    near_terms = jnp.stack([near_k, near_v], 0).reshape(2, local_count, HEADS, 3, BLOCK, HEAD_DIM)
    padded_grads = jnp.zeros((2, local_count + 2, HEADS, BLOCK, HEAD_DIM), f32)
    for offset in range(3):
        padded_grads = padded_grads.at[:, offset : offset + local_count].add(
            near_terms[:, :, :, offset]
        )
    lower_rim = padded_grads[:, 0]
    upper_rim = padded_grads[:, local_count + 1]
    local_grads = padded_grads[:, 1 : local_count + 1]
    from_above = passed_along(lower_rim.astype(jnp.bfloat16), "seq", -1).astype(lower_rim.dtype)
    from_below = passed_along(upper_rim.astype(jnp.bfloat16), "seq", 1).astype(upper_rim.dtype)
    local_grads = local_grads.at[:, 0].add(from_below)
    local_grads = local_grads.at[:, local_count - 1].add(from_above)
    glob_k = score_scale * jnp.einsum(
        "jhqk,jhqe->hke",
        grad_scores[..., n_near : n_near + n_glob],
        q_heads,
        preferred_element_type=f32,
    )
    glob_v = jnp.einsum(
        "jhqk,jhqe->hke",
        probs_b[..., n_near : n_near + n_glob],
        d_heads,
        preferred_element_type=f32,
    )
    glob_terms = jnp.stack([glob_k, glob_v], 0).reshape(2, HEADS, GLOBALS, BLOCK, HEAD_DIM)
    glob_terms = jnp.transpose(glob_terms, (0, 2, 1, 3, 4))
    glob_sum = lax.psum(glob_terms, "seq")
    global_hit = (
        global_blocks[:, None]
        == own_index * local_count + jnp.arange(local_count, dtype=jnp.int32)[None, :]
    ).astype(f32)
    local_grads = local_grads + jnp.einsum(
        "gj,cghke->cjhke", global_hit, glob_sum, precision=lax.Precision.HIGHEST
    )
    rand_k = (
        score_scale
        * jnp.einsum(
            "jhqk,jhqe->jhke",
            grad_scores[..., n_near + n_glob :],
            q_heads,
            preferred_element_type=f32,
        )
    ).astype(jnp.bfloat16)
    rand_v = jnp.einsum(
        "jhqk,jhqe->jhke", probs_b[..., n_near + n_glob :], d_heads, preferred_element_type=f32
    ).astype(jnp.bfloat16)
    rand_terms = jnp.stack([rand_k, rand_v], 2).reshape(
        local_count, HEADS, 2, RANDOM, BLOCK, HEAD_DIM
    )
    rand_items = jnp.transpose(rand_terms, (1, 0, 3, 2, 4, 5)).reshape(requests, 2, BLOCK, HEAD_DIM)
    back_send = jnp.zeros((shards, capacity, 2, BLOCK, HEAD_DIM), jnp.bfloat16)
    back_send = back_send.at[owner_of, slot_rank].set(rand_items)
    returned = lax.all_to_all(back_send, "seq", split_axis=0, concat_axis=0, tiled=True)
    gained = jnp.where(filled[:, :, None, None, None] > 0, returned.astype(f32), 0.0)
    local_grads = local_grads.at[:, code_block, code_head].add(jnp.moveaxis(gained, 2, 0))
    rows = queries.shape[0]
    width = queries.shape[1]
    grads_rows = jnp.transpose(local_grads, (0, 1, 3, 2, 4)).reshape(2, rows, width)
    return (
        jnp.transpose(attended, (0, 2, 1, 3)).astype(jnp.bfloat16).reshape(rows, width),
        jnp.transpose(grad_q, (0, 2, 1, 3)).astype(jnp.bfloat16).reshape(rows, width),
        grads_rows[0].astype(jnp.bfloat16),
        grads_rows[1].astype(jnp.bfloat16),
    )


def solution(mesh):
    return jax.shard_map(
        on_device,
        mesh=mesh,
        in_specs=(
            P(("groups", "seq"), None),
            P(("groups", "seq"), None),
            P(("groups", "seq"), None),
            P(("groups", "seq"), None),
            P("groups"),
            P("groups", None, None),
        ),
        out_specs=(
            P(("groups", "seq"), None),
            P(("groups", "seq"), None),
            P(("groups", "seq"), None),
            P(("groups", "seq"), None),
        ),
        check_vma=False,
    )
```

profile of v0, /device:TPU:25, one launch (start us, length us, event | category | flops | bytes accessed | tf_op | source)
XLA Modules:
  0.0 628.8 jit_solution(2648238937101494950)
XLA Ops:
  13.6 9.4 %gather_fusion = bf16[192,2,64,128]{3,2,1,0:T(8,128)(2,1)} fusion(bf16[2,4,64,16,128]{4,2,3,1,0:T(8,128)(2,1)S(1)} %copy_dynamic-update-slice_fusion, s32[192]{0:T(256)S(1)} %reshape.547), kind=kCustom, calls=%fused_computation | custom fusion | bytes 12584448 | tf_op jit(solution)/shard_map/gather | solution.py:78
  23.0 5.9 broadcast_select_fusion
  29.0 6.5 %all-to-all-start = ((bf16[16,12,2,64,128]{4,3,2,1,0:T(8,128)(2,1)}), bf16[16,12,2,64,128]{4,3,2,1,0:T(8,128)(2,1)}, u32[]{:S(2)}, u32[]{:S(2)}) async-start(bf16[16,12,2,64,128]{4,3,2,1,0:T(8,128)(2,1)} %broadcast_select_fusion), calls=%async_computation | async-start | bytes 12582912 | tf_op jit(solution)/shard_map/all_to_all | solution.py:80
  39.9 3.5 collective-permute-start
  55.6 172.4 %all-reduce.10.cloned.1.call-done = (bf16[2,1,64,16,128]{4,2,3,1,0:T(8,128)(2,1)}, bf16[2,1,64,16,128]{4,2,3,1,0:T(8,128)(2,1)}) async-done(((bf16[2,1,64,16,128]{4,2,3,1,0:T(8,128)(2,1)}, bf16[2,1,64,16,128]{4,2,3,1,0:T(8,128)(2,1)}), (bf16[2,1,64,16,128]{4,2,3,1,0:T(8,128)(2,1)}, bf16[2,1,64,16,128]{4,2,3,1,0:T(8,128)(2,1)})) %all-reduce.10.cloned.1.call-update) | async-done | bytes 1048592 | tf_op jit(solution)/shard_map/psum | solution.py:33
  235.4 3.3 pad_maximum_fusion.1
  238.7 12.2 %gather_fusion.1 = bf16[192,2,64,128]{3,2,1,0:T(8,128)(2,1)} fusion(bf16[16,12,2,64,128]{4,3,2,1,0:T(8,128)(2,1)} %all-to-all-done, s32[192]{0:T(256)S(1)} %bitcast.250), kind=kCustom, calls=%fused_computation.1 | custom fusion | bytes 12584448 | tf_op jit(solution)/shard_map/gather | solution.py:81
  250.9 4.5 copy.156
  256.5 6.9 %pad_maximum_fusion = bf16[2,4,16,512,128]{4,3,2,1,0:T(8,128)(2,1)} fusion(bf16[2,4,16,192,128]{4,3,2,1,0:T(8,128)(2,1)S(1)} %bitcast.234, bf16[2,4,16,128,128]{4,3,2,1,0:T(8,128)(2,1)S(1)} %broadcast_in_dim.41, bf16[2,4,16,192,128]{4,3,2,1,0:T(8,128)(2,1)S(1)} %bitcast.233), kind=kLoop, calls=%fused_computation.5 | loop fusion | flops 50331648 | bytes 33554432 | tf_op jit(solution)/shard_map/concatenate | solution.py:103
  263.5 9.6 %fusion.7 = f32[4,16,512,64]{2,3,1,0:T(8,128)} fusion(bf16[2,4,16,512,128]{4,3,2,1,0:T(8,128)(2,1)} %pad_maximum_fusion, bf16[4,64,16,128]{3,2,1,0:T(8,128)(2,1)S(1)} %bitcast.240), kind=kOutput, calls=%fused_computation.24 | convolution fusion | flops 536870912 | bytes 17825792 | tf_op jit(solution)/shard_map/jhqe,jhke->jhqk/dot_general | solution.py:118
  273.1 11.5 %fusion.75 = (f32[4,16,64]{2,1,0:T(8,128)S(1)}, f32[4,16,64,512]{3,2,1,0:T(8,128)}) fusion(f32[4,16,512,64]{2,3,1,0:T(8,128)} %fusion.7, pred[4,512]{1,0:T(4,128)(4,1)S(1)} %concatenate.31), kind=kOutput, calls=%fused_computation.177 | output fusion | flops 12583423 | bytes 16795648 | tf_op jit(solution)/shard_map/sub | solution.py:122
  284.6 9.4 %fusion.1 = (f32[4,16,64]{2,1,0:T(8,128)S(1)}, f32[4,16,512,64]{2,3,1,0:T(8,128)}) fusion(f32[4,16,64,512]{3,2,1,0:T(8,128)} %get-tuple-element.92, f32[4,16,64]{2,1,0:T(8,128)S(1)} %get-tuple-element.91, bf16[4,64,16,128]{3,2,1,0:T(8,128)(2,1)S(1)} %bitcast.257, bf16[2,4,16,512,128]{4,3,2,1,0:T(8,128)(2,1)} %pad_maximum_fusion), kind=kOutput, calls=%fused_computation.15 | convolution fusion | flops 543158272 | bytes 26247168 | tf_op jit(solution)/shard_map/jhqe,jhke->jhqk/dot_general | solution.py:127
  294.0 7.1 %fusion.3 = (bf16[4,16,64,512]{3,2,1,0:T(8,128)(2,1)S(1)}, bf16[4,16,64,512]{3,2,1,0:T(8,128)(2,1)S(1)}) fusion(f32[4,16,512,64]{2,3,1,0:T(8,128)} %get-tuple-element.94, f32[4,16,64]{2,1,0:T(8,128)S(1)} %get-tuple-element.93, f32[4,16,64,512]{3,2,1,0:T(8,128)} %get-tuple-element.92, f32[4,16,64]{2,1,0:T(8,128)S(1)} %get-tuple-element.91), kind=kLoop, calls=%fused_computation.17 | loop fusion | flops 10485760 | bytes 25198592 | tf_op jit(solution)/shard_map/convert_element_type | solution.py:129
  306.5 4.2 copy.174
  310.7 4.2 broadcast.408
  314.9 30.9 %scatter_fusion = bf16[16,12,2,64,128]{4,3,2,1,0:T(8,128)(2,1)} fusion(bf16[16,12,2,64,128]{4,3,2,1,0:T(8,128)(2,1)} %broadcast.408, s32[192]{0:T(256)S(1)} %bitcast.249, bf16[192,2,64,128]{3,2,1,0:T(8,128)(2,1)} %bitcast.236), kind=kCustom, calls=%fused_computation.2 | custom fusion | bytes 18875904 | tf_op jit(solution)/shard_map/scatter | solution.py:191
  345.8 7.8 %all-to-all-start.1 = ((bf16[16,12,2,64,128]{4,3,2,1,0:T(8,128)(2,1)}), bf16[16,12,2,64,128]{4,3,2,1,0:T(8,128)(2,1)}, u32[]{:S(2)}, u32[]{:S(2)}) async-start(bf16[16,12,2,64,128]{4,3,2,1,0:T(8,128)(2,1)} %scatter_fusion), calls=%async_computation.1 | async-start | bytes 12582912 | tf_op jit(solution)/shard_map/all_to_all | solution.py:192
  353.7 2.8 fusion.21
  357.7 3.4 pad_maximum_fusion.3
  368.5 3.3 collective-permute-start.2
  374.6 2.6 fusion.28
  378.1 2.6 fusion.26
  384.0 6.4 %fusion.27 = bf16[4,64,16,128]{3,1,2,0:T(8,128)(2,1)S(1)} fusion(bf16[4,16,64,512]{3,2,1,0:T(8,128)(2,1)} %copy-done.3, bf16[2,4,16,512,128]{4,3,2,1,0:T(8,128)(2,1)} %pad_maximum_fusion), kind=kOutput, calls=%fused_computation.64 | convolution fusion | flops 537919488 | bytes 13631488 | tf_op jit(solution)/shard_map/jhqk,jhke->jhqe/dot_general | solution.py:130
  390.5 5.5 fusion.25
  401.4 5.8 copy.164
  409.6 26.5 %scatter-add.36 = f32[2,4,16,64,128]{4,1,3,2,0:T(4,128)} dynamic-update-slice(f32[2,4,16,64,128]{4,1,3,2,0:T(4,128)} %copy.164, f32[2,1,16,64,128]{4,1,3,2,0:T(1,128)S(1)} %add.195, s32[]{:T(128)} %constant.236.clone.1, s32[]{:T(128)} %constant.240.clone.1, s32[]{:T(128)} %constant.236.clone.1, s32[]{:T(128)} %constant.236.clone.1, s32[]{:T(128)} %constant.236.clone.1) | dynamic-update-slice | bytes 2097156 | tf_op jit(solution)/shard_map/scatter-add | solution.py:151
  436.0 119.9 %all-reduce.8.cloned.1.call-done = f32[2,2,16,64,128]{4,1,3,2,0:T(2,128)} async-done(((f32[2,2,16,64,128]{4,1,3,2,0:T(2,128)}), f32[2,2,16,64,128]{4,1,3,2,0:T(2,128)}) %all-reduce.8.cloned.1.call-update) | async-done | bytes 2097168 | tf_op jit(solution)/shard_map/psum | solution.py:166
  555.9 7.5 %bitcast_add_fusion = f32[2,4,16,64,128]{4,1,3,2,0:T(4,128)S(1)} fusion(f32[2,4,16,64,128]{4,1,3,2,0:T(4,128)} %scatter-add.36, f32[2,2,16,64,128]{4,1,3,2,0:T(2,128)} %all-reduce.8.cloned.1.call-done, s32[4]{0:T(128)S(1)} %iota_add_fusion, s32[2]{0:T(128)S(1)} %copy-done.9), kind=kOutput, calls=%fused_computation.40 | convolution fusion | flops 26214408 | bytes 10485784 | tf_op jit(solution)/shard_map/gj,cghke->cjhke/dot_general | solution.py:171
  563.4 2.5 copy.169
  565.9 8.3 %convert_select_fusion = f32[16,12,2,64,128]{4,3,2,1,0:T(8,128)} fusion(bf16[16,12,2,64,128]{4,3,2,1,0:T(8,128)(2,1)} %all-to-all-done.1, pred[16,12]{1,0:T(8,128)(4,1)S(1)} %copy.149), kind=kLoop, calls=%fused_computation.10 | loop fusion | flops 6291456 | bytes 18874560 | tf_op jit(solution)/shard_map/jit(_where)/select_n | solution.py:193
  574.2 40.7 %scatter_fusion.1 = f32[2,4,16,64,128]{4,3,2,1,0:T(8,128)} fusion(f32[2,4,16,64,128]{4,3,2,1,0:T(8,128)} %copy.169, s32[192]{0:T(256)S(1)} %reshape.565, f32[192,2,64,128]{3,2,1,0:T(8,128)} %bitcast.229), kind=kCustom, calls=%fused_computation.3 | custom fusion | flops 3145728 | bytes 37750272 | tf_op jit(solution)/shard_map/scatter-add | solution.py:194
  614.9 2.7 convert_bitcast_fusion
  (125 shorter events, 58.7 us)
Async XLA Ops:
  7.2 3.2 copy-start.8
  29.0 6.5 %copy-start.5 = (bf16[256,2048]{1,0:T(8,128)(2,1)S(1)}, bf16[256,2048]{1,0:T(8,128)(2,1)}, u32[]{:S(2)}) copy-start(bf16[256,2048]{1,0:T(8,128)(2,1)} %param.17) | copy-start | bytes 3145732
  29.0 14.4 %copy-start.9 = (s32[2]{0:T(128)S(1)}, s32[2]{0:T(128)}, u32[]{:S(2)}) copy-start(s32[2]{0:T(128)} %param.20) | copy-start | bytes 28
  29.0 209.8 %all-to-all-start = ((bf16[16,12,2,64,128]{4,3,2,1,0:T(8,128)(2,1)}), bf16[16,12,2,64,128]{4,3,2,1,0:T(8,128)(2,1)}, u32[]{:S(2)}, u32[]{:S(2)}) async-start(bf16[16,12,2,64,128]{4,3,2,1,0:T(8,128)(2,1)} %broadcast_select_fusion), calls=%async_computation | async-start | bytes 12582912 | tf_op jit(solution)/shard_map/all_to_all | solution.py:80
  35.5 192.5 %all-reduce.10.cloned.1.call-start = ((), (), s32[]{:S(2)}) async-start(), calls=%async_computation.3 | async-start | bytes 2097152 | tf_op jit(solution)/shard_map/psum | solution.py:33
  37.6 192.7 %collective-permute-start.1 = (bf16[2,64,2048]{2,1,0:T(8,128)(2,1)}, bf16[2,64,2048]{2,1,0:T(8,128)(2,1)}, u32[]{:S(2)}, u32[]{:S(2)}) collective-permute-start(bf16[2,64,2048]{2,1,0:T(8,128)(2,1)} %get-tuple-element.84), channel_id=1, source_target_pairs={{1,0},{2,1},{3,2},{4,3},{5,4},{6,5},{7,6},{8,7},{9,8},{10,9},{11,1... | collective-permute-start | bytes 1572872 | tf_op jit(solution)/shard_map/ppermute | solution.py:26
  39.9 190.4 %collective-permute-start = (bf16[2,64,2048]{2,1,0:T(8,128)(2,1)}, bf16[2,64,2048]{2,1,0:T(8,128)(2,1)}, u32[]{:S(2)}, u32[]{:S(2)}) collective-permute-start(bf16[2,64,2048]{2,1,0:T(8,128)(2,1)} %get-tuple-element.83), channel_id=1, source_target_pairs={{0,1},{1,2},{2,3},{3,4},{4,5},{5,6},{6,7},{7,8},{8,9},{9,10},{10,1... | collective-permute-start | bytes 1572872 | tf_op jit(solution)/shard_map/ppermute | solution.py:25
  250.9 5.6 slice-start.2
  250.9 4.5 copy-start.7
  250.9 5.6 slice-start.3
  273.1 11.5 %copy-start.6 = (bf16[32,8,16,128]{3,2,1,0:T(8,128)(2,1)S(1)}, bf16[32,8,16,128]{3,2,1,0:T(8,128)(2,1)}, u32[]{:S(2)}) copy-start(bf16[32,8,16,128]{3,2,1,0:T(8,128)(2,1)} %copy.187) | copy-start | bytes 3145732
  301.1 4.8 copy-start.1
  301.1 4.8 copy-start.3
  345.8 220.1 %all-to-all-start.1 = ((bf16[16,12,2,64,128]{4,3,2,1,0:T(8,128)(2,1)}), bf16[16,12,2,64,128]{4,3,2,1,0:T(8,128)(2,1)}, u32[]{:S(2)}, u32[]{:S(2)}) async-start(bf16[16,12,2,64,128]{4,3,2,1,0:T(8,128)(2,1)} %scatter_fusion), calls=%async_computation.1 | async-start | bytes 12582912 | tf_op jit(solution)/shard_map/all_to_all | solution.py:192
  353.6 202.3 %all-reduce.8.cloned.1.call-start = ((), (), s32[]{:S(2)}) async-start(), calls=%async_computation.2 | async-start | bytes 4194304 | tf_op jit(solution)/shard_map/psum | solution.py:166
  353.7 2.8 copy-start.4
  367.6 14.0 %copy-start = (f32[2,6,16,64,128]{4,3,2,0,1:T(8,128)}, f32[2,6,16,64,128]{4,3,2,0,1:T(8,128)S(1)}, u32[]{:S(2)}) copy-start(f32[2,6,16,64,128]{4,3,2,0,1:T(8,128)S(1)} %get-tuple-element.71) | copy-start | bytes 18874372
  368.5 31.7 %collective-permute-start.2 = (bf16[2,16,64,128]{3,2,1,0:T(8,128)(2,1)}, bf16[2,16,64,128]{3,2,1,0:T(8,128)(2,1)}, u32[]{:S(2)}, u32[]{:S(2)}) collective-permute-start(bf16[2,16,64,128]{3,2,1,0:T(8,128)(2,1)} %fusion.48), channel_id=1, source_target_pairs={{0,1},{1,2},{2,3},{3,4},{4,5},{5,6},{6,7},{7,8},{8,9},{9,10},{10,1... | collective-permute-start | bytes 1572872 | tf_op jit(solution)/shard_map/ppermute | solution.py:39
  372.7 34.6 %collective-permute-start.3 = (bf16[2,16,64,128]{3,2,1,0:T(8,128)(2,1)}, bf16[2,16,64,128]{3,2,1,0:T(8,128)(2,1)}, u32[]{:S(2)}, u32[]{:S(2)}) collective-permute-start(bf16[2,16,64,128]{3,2,1,0:T(8,128)(2,1)} %fusion.49), channel_id=1, source_target_pairs={{1,0},{2,1},{3,2},{4,3},{5,4},{6,5},{7,6},{8,7},{9,8},{10,9},{11,1... | collective-permute-start | bytes 1572872 | tf_op jit(solution)/shard_map/ppermute | solution.py:39
  384.0 12.0 %slice-start = ((s8[6291456]{0:T(1024)(128)(4,1)}), s8[2097152]{0:T(1024)(128)(4,1)S(1)}, s32[]{:S(2)}) async-start(s8[6291456]{0:T(1024)(128)(4,1)} %bitcast.227), calls=%async_computation.4 | async-start | bytes 4194304
  384.0 6.5 %copy-start.2 = (bf16[4,16,64,512]{3,2,1,0:T(8,128)(2,1)S(1)}, bf16[4,16,64,512]{3,2,1,0:T(8,128)(2,1)}, u32[]{:S(2)}) copy-start(bf16[4,16,64,512]{3,2,1,0:T(8,128)(2,1)} %copy-done.1) | copy-start | bytes 12582916
  384.0 12.0 %slice-start.1 = ((s8[6291456]{0:T(1024)(128)(4,1)}), s8[4194304]{0:T(1024)(128)(4,1)S(1)}, s32[]{:S(2)}) async-start(s8[6291456]{0:T(1024)(128)(4,1)} %bitcast.227), calls=%async_computation.5 | async-start | bytes 8388608
Sparse Core Ops, SparseCore 0:
  50.4 177.4 all-reduce.9
  384.1 171.7 all-reduce.7
where the time goes:
time: 641 us; the launch traced here: 629 us
  waiting for transfers between devices  292 us (46%)
  local copies, waits for them, and re-layouts  130 us (20%)
  other arithmetic  108 us (17%)
  matrix products  52.4 us (8%)
  starting transfers between devices  25.4 us (4%)
  between operations  20.3 us (3%)
    psum x1, waiting for transfers between devices, from_root(): return lax.psum(kept, axis)  172 us
    psum x1, waiting for transfers between devices, on_device(): glob_sum = lax.psum(glob_terms, 'seq')  120 us
    scatter-add x1, other arithmetic, on_device(): local_grads.at[:, code_block, code_head].add(jnp.moveaxis(gained, 2, 0))  40.7 us
    scatter x1, local copies, waits for them, and re-layouts, on_device(): back_send = back_send.at[owner_of, slot_rank].set(rand_items)  30.9 us
    scatter-add x1, local copies, waits for them, and re-layouts, on_device(): local_grads = local_grads.at[:, local_count - 1].add(from_above)  26.5 us
    unnamed x40, local copies, waits for them, and re-layouts  15.7 us
  transfers between devices with their start and end apart: 8, of which 2 were waited for; matrix products, arithmetic and copies ran while one was open for 17% of the time, Pallas kernels for 0%

commit v1 on v0

v1 whole, which is shorter than its diff:
```python
import functools
import math

import jax
import jax.numpy as jnp
from jax import lax
from jax.experimental import pallas as pl
from jax.experimental.pallas import tpu as pltpu
from jax.sharding import PartitionSpec as P

HEADS = 16
HEAD_DIM = 128
BLOCK = 64
GLOBALS = 2
RANDOM = 3
MASKED = -1e30
MESH = pl.DeviceIdType.MESH
ANY = pl.BlockSpec(memory_space=pl.ANY)
VMEM = pl.BlockSpec(memory_space=pltpu.VMEM)
SMEM = pl.BlockSpec(memory_space=pltpu.SMEM)
VMEM_LIMIT = 48 * 1024 * 1024


def enter(me, shards):
    barrier = pltpu.get_barrier_semaphore()

    def greet(step, carry):
        pl.semaphore_signal(
            barrier, inc=1, device_id={"seq": lax.rem(me + step, shards)}, device_id_type=MESH
        )
        return carry

    lax.fori_loop(1, shards, greet, 0)
    pl.semaphore_wait(barrier, shards - 1)


def remote(src, dst, sems, slot, target):
    return pltpu.make_async_remote_copy(
        src_ref=src,
        dst_ref=dst,
        send_sem=sems[0].at[slot],
        recv_sem=sems[1].at[slot],
        device_id={"seq": target},
        device_id_type=MESH,
    )


def fetch_kernel(shards, capacity, code, k, v, got, before, after, tiles, staged, send, recv, rim_send, rim_recv, own):
    me = lax.axis_index("seq")
    up, down = lax.rem(me + 1, shards), lax.rem(me + shards - 1, shards)
    rows = k.shape[0]
    last = pl.ds(rows - BLOCK, BLOCK)
    initial = pl.ds(0, BLOCK)
    for which, ref in enumerate((k, v)):
        for block in range(rows // BLOCK):
            for head in range(HEADS):
                tiles[block * HEADS + head, which] = ref[
                    block * BLOCK : (block + 1) * BLOCK, head * HEAD_DIM : (head + 1) * HEAD_DIM
                ]
    enter(me, shards)
    rims = []
    for which, ref in enumerate((k, v)):
        rims.append(remote(ref.at[last], before.at[which], (rim_send, rim_recv), which, up))
        rims.append(remote(ref.at[initial], after.at[which], (rim_send, rim_recv), 2 + which, down))

    def gather(target):
        def item(slot, carry):
            staged[target, slot] = tiles[code[target * capacity + slot]]
            return carry

        lax.fori_loop(0, capacity, item, 0)

    def give(step, carry):
        target = lax.rem(me + step, shards)
        gather(target)
        remote(staged.at[target], got.at[me], (send, recv), step, target).start()
        return carry

    lax.fori_loop(1, shards, give, 0)
    for rim in rims:
        rim.start()
    gather(me)
    mine = pltpu.make_async_copy(staged.at[me], got.at[me], own)
    mine.start()
    mine.wait()
    for rim in rims:
        rim.wait()

    def finish(step, carry):
        target = lax.rem(me + step, shards)
        source = lax.rem(me + shards - step, shards)
        remote(staged.at[target], got.at[source], (send, recv), step, target).wait()
        return carry

    lax.fori_loop(1, shards, finish, 0)


def fetch(code, keys, values, shards, capacity):
    kind = jnp.bfloat16
    width = keys.shape[1]
    return pl.pallas_call(
        functools.partial(fetch_kernel, shards, capacity),
        out_shape=(
            jax.ShapeDtypeStruct((shards, capacity, 2, BLOCK, HEAD_DIM), kind),
            jax.ShapeDtypeStruct((2, BLOCK, width), kind),
            jax.ShapeDtypeStruct((2, BLOCK, width), kind),
        ),
        in_specs=[SMEM, VMEM, VMEM],
        out_specs=(ANY, ANY, ANY),
        scratch_shapes=[
            pltpu.VMEM((keys.shape[0] // BLOCK * HEADS, 2, BLOCK, HEAD_DIM), kind),
            pltpu.VMEM((shards, capacity, 2, BLOCK, HEAD_DIM), kind),
            pltpu.SemaphoreType.DMA((shards,)),
            pltpu.SemaphoreType.DMA((shards,)),
            pltpu.SemaphoreType.DMA((4,)),
            pltpu.SemaphoreType.DMA((4,)),
            pltpu.SemaphoreType.DMA,
        ],
        compiler_params=pltpu.CompilerParams(
            collective_id=0, has_side_effects=True, vmem_limit_bytes=VMEM_LIMIT
        ),
        cost_estimate=pl.CostEstimate(flops=0, bytes_accessed=300_000_000, transcendentals=0),
        name="fetch",
    )(code, keys, values)


def give_back_kernel(shards, back, lower, upper, got, above, below, send, recv, rim_send, rim_recv, own):
    me = lax.axis_index("seq")
    up, down = lax.rem(me + 1, shards), lax.rem(me + shards - 1, shards)
    enter(me, shards)
    rims = [
        remote(lower, above, (rim_send, rim_recv), 0, down),
        remote(upper, below, (rim_send, rim_recv), 1, up),
    ]

    def give(step, carry):
        target = lax.rem(me + step, shards)
        remote(back.at[target], got.at[me], (send, recv), step, target).start()
        return carry

    lax.fori_loop(1, shards, give, 0)
    for rim in rims:
        rim.start()
    mine = pltpu.make_async_copy(back.at[me], got.at[me], own)
    mine.start()
    mine.wait()
    for rim in rims:
        rim.wait()

    def finish(step, carry):
        target = lax.rem(me + step, shards)
        source = lax.rem(me + shards - step, shards)
        remote(back.at[target], got.at[source], (send, recv), step, target).wait()
        return carry

    lax.fori_loop(1, shards, finish, 0)


def give_back(back, lower, upper, shards):
    return pl.pallas_call(
        functools.partial(give_back_kernel, shards),
        out_shape=tuple(jax.ShapeDtypeStruct(a.shape, a.dtype) for a in (back, lower, upper)),
        in_specs=[ANY, ANY, ANY],
        out_specs=(ANY, ANY, ANY),
        scratch_shapes=[
            pltpu.SemaphoreType.DMA((shards,)),
            pltpu.SemaphoreType.DMA((shards,)),
            pltpu.SemaphoreType.DMA((2,)),
            pltpu.SemaphoreType.DMA((2,)),
            pltpu.SemaphoreType.DMA,
        ],
        compiler_params=pltpu.CompilerParams(collective_id=1, has_side_effects=True),
        cost_estimate=pl.CostEstimate(flops=0, bytes_accessed=300_000_000, transcendentals=0),
        name="give_back",
    )(back, lower, upper)


def dot(a, b, dims):
    return lax.dot_general(a, b, (dims, ((), ())), preferred_element_type=jnp.float32)


def attend_kernel(blocks, place, owner, rank, q, d, k, v, before, after, glob, *rest):
    items = blocks * RANDOM
    rand = rest[:items]
    attended, grad_q, own_grad, lower, upper, glob_grad, back, near, terms, sems = rest[items:]
    head = pl.program_id(0)
    heads = pl.num_programs(0)
    slot = lax.rem(head, 2)
    scale = 1.0 / math.sqrt(HEAD_DIM)
    n_near = 3 * BLOCK
    n_glob = GLOBALS * BLOCK
    f32, b16 = jnp.float32, jnp.bfloat16

    def out_copy(at_head, at_slot, item):
        index = at_head * items + item
        return pltpu.make_async_copy(
            terms.at[at_slot, item], back.at[owner[index], rank[index]], sems.at[at_slot, item]
        )

    @pl.when(head >= 2)
    def _():
        for item in range(items):
            out_copy(head - 2, slot, item).wait()

    near[...] = jnp.zeros_like(near)
    k_all = jnp.concatenate([before[0], k[...], after[0]], 0)
    v_all = jnp.concatenate([before[1], v[...], after[1]], 0)
    gk, gv = glob[0], glob[1]
    glob_k = jnp.zeros((n_glob, HEAD_DIM), f32)
    glob_v = jnp.zeros((n_glob, HEAD_DIM), f32)
    for j in range(blocks):
        rows = pl.ds(j * BLOCK, BLOCK)
        span = slice(j * BLOCK, j * BLOCK + n_near)
        qj, dj = q[rows, :], d[rows, :]
        picked = [rand[j * RANDOM + r] for r in range(RANDOM)]
        kj = jnp.concatenate([k_all[span], gk] + [x[0, 0, 0] for x in picked], 0)
        vj = jnp.concatenate([v_all[span], gv] + [x[0, 0, 1] for x in picked], 0)
        s = dot(qj, kj, ((1,), (1,))) * scale
        if j == 0 or j == blocks - 1:
            column = lax.broadcasted_iota(jnp.int32, s.shape, 1)
            if j == 0:
                s = jnp.where((column < BLOCK) & (place[0] == 0), MASKED, s)
            if j == blocks - 1:
                outside = (column >= 2 * BLOCK) & (column < n_near) & (place[1] == 0)
                s = jnp.where(outside, MASKED, s)
        e = jnp.exp(s - jnp.max(s, -1, keepdims=True))
        p = e * (1.0 / jnp.sum(e, -1, keepdims=True))
        pb = p.astype(b16)
        attended[rows, :] = dot(pb, vj, ((1,), (0,))).astype(b16)
        gp = dot(dj, vj, ((1,), (1,)))
        delta = jnp.sum(p * gp, -1, keepdims=True)
        ds = (p * (gp - delta)).astype(b16)
        grad_q[rows, :] = (scale * dot(ds, kj, ((1,), (0,)))).astype(b16)
        dk = scale * dot(ds, qj, ((0,), (0,)))
        dv = dot(pb, dj, ((0,), (0,)))
        near[0, span] += dk[:n_near]
        near[1, span] += dv[:n_near]
        glob_k += dk[n_near : n_near + n_glob]
        glob_v += dv[n_near : n_near + n_glob]
        for r in range(RANDOM):
            item = j * RANDOM + r
            at = slice(n_near + n_glob + r * BLOCK, n_near + n_glob + (r + 1) * BLOCK)
            terms[slot, item, 0] = dk[at].astype(b16)
            terms[slot, item, 1] = dv[at].astype(b16)
            out_copy(head, slot, item).start()
    glob_grad[0] = glob_k
    glob_grad[1] = glob_v
    own_grad[...] = near[:, BLOCK : (blocks + 1) * BLOCK]
    lower[...] = near[:, :BLOCK].astype(b16)
    upper[...] = near[:, (blocks + 1) * BLOCK :].astype(b16)

    @pl.when(head == heads - 1)
    def _():
        for item in range(items):
            out_copy(head - 1, 1 - slot, item).wait()
        for item in range(items):
            out_copy(head, slot, item).wait()


def attend(place, owner, rank, q, d, k, v, before, after, glob, got):
    rows, width = q.shape
    blocks = rows // BLOCK
    items = blocks * RANDOM
    f32, b16 = jnp.float32, jnp.bfloat16

    def flat():
        return pl.BlockSpec((rows, HEAD_DIM), lambda h, *_: (0, h))

    def pair(n):
        return pl.BlockSpec((2, n, HEAD_DIM), lambda h, *_: (0, 0, h))

    def picked(item):
        def at(h, place, owner, rank):
            return (owner[h * items + item], rank[h * items + item], 0, 0, 0)

        return pl.BlockSpec((1, 1, 2, BLOCK, HEAD_DIM), at)

    n_glob = GLOBALS * BLOCK
    return pl.pallas_call(
        functools.partial(attend_kernel, blocks),
        grid_spec=pltpu.PrefetchScalarGridSpec(
            num_scalar_prefetch=3,
            grid=(HEADS,),
            in_specs=[flat(), flat(), flat(), flat(), pair(BLOCK), pair(BLOCK), pair(n_glob)]
            + [picked(item) for item in range(items)],
            out_specs=[flat(), flat(), pair(rows), pair(BLOCK), pair(BLOCK), pair(n_glob), ANY],
            scratch_shapes=[
                pltpu.VMEM((2, rows + 2 * BLOCK, HEAD_DIM), f32),
                pltpu.VMEM((2, items, 2, BLOCK, HEAD_DIM), b16),
                pltpu.SemaphoreType.DMA((2, items)),
            ],
        ),
        out_shape=(
            jax.ShapeDtypeStruct((rows, width), b16),
            jax.ShapeDtypeStruct((rows, width), b16),
            jax.ShapeDtypeStruct((2, rows, width), f32),
            jax.ShapeDtypeStruct((2, BLOCK, width), b16),
            jax.ShapeDtypeStruct((2, BLOCK, width), b16),
            jax.ShapeDtypeStruct((2, n_glob, width), f32),
            jax.ShapeDtypeStruct(got.shape, b16),
        ),
        compiler_params=pltpu.CompilerParams(vmem_limit_bytes=VMEM_LIMIT),
        name="attend",
    )(place, owner, rank, q, d, k, v, before, after, glob, *([got] * items))


def combine_kernel(capacity, blocks, code, place, hit, own, above, below, glob, got, grad_k, grad_v, acc):
    source = pl.program_id(0)
    rows = blocks * BLOCK

    @pl.when(source == 0)
    def _():
        acc[...] = own[...]

        @pl.when(place[0] > 0)
        def _():
            acc[:, :BLOCK] += below[...].astype(jnp.float32)

        @pl.when(place[1] > 0)
        def _():
            acc[:, rows - BLOCK :] += above[...].astype(jnp.float32)

        for g in range(GLOBALS):

            @pl.when(hit[g] >= 0)
            def _():
                at = pl.ds(pl.multiple_of(hit[g] * BLOCK, BLOCK), BLOCK)
                acc[:, at] += glob[:, g * BLOCK : (g + 1) * BLOCK]

    for slot in range(capacity):
        packed = code[source * capacity + slot]

        @pl.when(packed >= 0)
        def _():
            row = pl.ds(pl.multiple_of(packed // HEADS * BLOCK, BLOCK), BLOCK)
            column = pl.ds(pl.multiple_of(packed % HEADS * HEAD_DIM, HEAD_DIM), HEAD_DIM)
            acc[:, row, column] += got[0, slot].astype(jnp.float32)

    @pl.when(source == pl.num_programs(0) - 1)
    def _():
        grad_k[...] = acc[0].astype(jnp.bfloat16)
        grad_v[...] = acc[1].astype(jnp.bfloat16)


def combine(code, place, hit, own, above, below, glob, got):
    shards, capacity = got.shape[:2]
    rows, width = own.shape[1:]

    def whole(a):
        return pl.BlockSpec(a.shape, lambda s, *_: (0, 0, 0))

    out = pl.BlockSpec((rows, width), lambda s, *_: (0, 0))
    return pl.pallas_call(
        functools.partial(combine_kernel, capacity, rows // BLOCK),
        grid_spec=pltpu.PrefetchScalarGridSpec(
            num_scalar_prefetch=3,
            grid=(shards,),
            in_specs=[
                whole(own),
                whole(above),
                whole(below),
                whole(glob),
                pl.BlockSpec((1, capacity, 2, BLOCK, HEAD_DIM), lambda s, *_: (s, 0, 0, 0, 0)),
            ],
            out_specs=[out, out],
            scratch_shapes=[pltpu.VMEM((2, rows, width), jnp.float32)],
        ),
        out_shape=(
            jax.ShapeDtypeStruct((rows, width), jnp.bfloat16),
            jax.ShapeDtypeStruct((rows, width), jnp.bfloat16),
        ),
        compiler_params=pltpu.CompilerParams(vmem_limit_bytes=VMEM_LIMIT),
        name="combine",
    )(code, place, hit, own, above, below, glob, got)


def on_device(queries, keys, values, grad_out, global_blocks, random_blocks):
    shards = lax.axis_size("seq")
    me = lax.axis_index("seq")
    blocks = queries.shape[0] // BLOCK
    i32 = jnp.int32

    mine = global_blocks // blocks == me
    parts = []
    for g in range(GLOBALS):
        start = global_blocks[g] % blocks * BLOCK
        pair = jnp.stack(
            [lax.dynamic_slice_in_dim(a, start, BLOCK, 0) for a in (keys, values)], 0
        )
        parts.append(jnp.where(mine[g], pair, jnp.zeros_like(pair)))
    glob = lax.psum(jnp.concatenate(parts, 1), "seq")

    wanted = lax.dynamic_slice_in_dim(random_blocks, me * blocks, blocks, 1).reshape(-1)
    requests = wanted.shape[0]
    capacity = (requests + shards - 1) // shards
    owner = wanted // blocks
    hits = (owner[:, None] == jnp.arange(shards, dtype=i32)[None, :]).astype(i32)
    rank = jnp.sum((jnp.cumsum(hits, 0) - hits) * hits, 1)
    asked = jnp.transpose(random_blocks.reshape(HEADS, shards, blocks, RANDOM), (1, 0, 2, 3))
    asked = asked.reshape(shards, requests)
    served = (asked // blocks == me).astype(i32)
    serve_rank = jnp.cumsum(served, 1) - served
    chosen = served[:, :, None] * (
        serve_rank[:, :, None] == jnp.arange(capacity, dtype=i32)[None, None, :]
    ).astype(i32)
    item_head = jnp.arange(requests, dtype=i32) // (blocks * RANDOM)
    entry = asked % blocks * HEADS + item_head[None, :] + 1
    code = (jnp.sum(chosen * entry[:, :, None], 1) - 1).reshape(-1)

    got, before, after = fetch(jnp.maximum(code, 0), keys, values, shards, capacity)
    place = jnp.stack([me, shards - 1 - me]).astype(i32)
    attended, grad_q, own_grad, lower, upper, glob_grad, back = attend(
        place, owner, rank, queries, grad_out, keys, values, before, after, glob, got
    )
    glob_sum = lax.psum(glob_grad, "seq")
    returned, above, below = give_back(back, lower, upper, shards)
    hit = jnp.where(mine, global_blocks % blocks, -1).astype(i32)
    grad_k, grad_v = combine(code, place, hit, own_grad, above, below, glob_sum, returned)
    return attended, grad_q, grad_k, grad_v


def solution(mesh):
    rows = P(("groups", "seq"), None)
    return jax.shard_map(
        on_device,
        mesh=mesh,
        in_specs=(rows, rows, rows, rows, P("groups"), P("groups", None, None)),
        out_specs=(rows, rows, rows, rows),
        check_vma=False,
    )
```

time: 641 us -> 541 us (0.84); the launches traced: 629 us -> 536 us
  Pallas kernels: 0 us -> 352 us
  waiting for transfers between devices: 292 us -> 147 us
  local copies, waits for them, and re-layouts: 130 us -> 14 us
  other arithmetic: 108 us -> 5.01 us
  matrix products: 52.4 us -> 0 us
  starting transfers between devices: 25.4 us -> 0.08 us
    pallas_call x0 -> x4, Pallas kernels: none -> 352 us  [the longest x1 144 us: give_back(): pl.pallas_call(functools.partial(give_back_kernel, shards), out_shape=tup...]
    psum x2, waiting for transfers between devices: 292 us -> 147 us  [the longest x1 78.2 us: on_device(): glob = lax.psum(jnp.concatenate(parts, 1), 'seq')]
    dot_general x11 -> x0, matrix products: 52.4 us -> none  [the longest x1 9.61 us: on_device(): jnp.einsum('jhqe,jhke->jhqk', q_heads, key_set[0], preferred_element_type...]
    scatter-add x4 -> x0, other arithmetic: 45.3 us -> none  [the longest x1 40.7 us: on_device(): local_grads.at[:, code_block, code_head].add(jnp.moveaxis(gained, 2, 0))]
    scatter-add x3 -> x0, local copies, waits for them, and re-layouts: 32.9 us -> none  [the longest x1 26.5 us: on_device(): local_grads = local_grads.at[:, local_count - 1].add(from_above)]
    scatter x1 -> x0, local copies, waits for them, and re-layouts: 30.9 us -> none  [on_device(): back_send = back_send.at[owner_of, slot_rank].set(rand_items)]
    gather x2 -> x0, local copies, waits for them, and re-layouts: 21.6 us -> none  [the longest x1 12.2 us: on_device(): fetched[owner_of, slot_rank]]
    all_to_all x2 -> x0, starting transfers between devices: 14.3 us -> none  [the longest x1 7.77 us: on_device(): lax.all_to_all(back_send, 'seq', split_axis=0, concat_axis=0, tiled=True)]
  transfers between devices with their start and end apart: 8 -> 2, of which waited for: 2 -> 2; matrix products, arithmetic and copies ran while one was open for 17% -> 1% of each run, Pallas kernels for 0% -> 52%
where the time goes in v1:
time: 541 us; the launch traced here: 536 us
  Pallas kernels  352 us (65%)
  waiting for transfers between devices  147 us (27%)
  between operations  18.2 us (3%)
  local copies, waits for them, and re-layouts  14 us (3%)
    pallas_call x1, Pallas kernels, give_back(): pl.pallas_call(functools.partial(give_back_kernel, shards), out_shape=tup...  144 us
    pallas_call x1, Pallas kernels, fetch(): pl.pallas_call(functools.partial(fetch_kernel, shards, capacity), out_sha...  137 us
    psum x1, waiting for transfers between devices, on_device(): glob = lax.psum(jnp.concatenate(parts, 1), 'seq')  78.2 us
    psum x1, waiting for transfers between devices, on_device(): glob_sum = lax.psum(glob_grad, 'seq')  68.3 us
    pallas_call x1, Pallas kernels, attend(): pl.pallas_call(functools.partial(attend_kernel, blocks), grid_spec=pltpu....  56.8 us
    pallas_call x1, Pallas kernels, combine(): pl.pallas_call(functools.partial(combine_kernel, capacity, rows // BLOCK)...  14.7 us
  transfers between devices with their start and end apart: 2, of which 2 were waited for; matrix products, arithmetic and copies ran while one was open for 1% of the time, Pallas kernels for 52%

profile of v1, /device:TPU:25, one launch (start us, length us, event | category | flops | bytes accessed | tf_op | source)
XLA Modules:
  0.0 536.0 jit_solution(13495289125844039408)
XLA Ops:
  7.2 1.3 fusion.13
  12.4 0.7 fusion.9
  13.1 0.6 fusion.12
  13.7 1.3 dynamic-slice_bitcast_fusion.2
  15.0 0.7 maximum_select_fusion
  15.7 0.7 maximum_select_fusion.1
  16.5 1.0 pad_maximum_fusion
  17.6 0.1 copy.50
  17.8 0.2 copy.47
  18.0 0.1 reshape.150
  18.2 0.6 reduce-window.14
  18.8 0.1 copy.51
  19.1 0.6 reduce-window.16
  19.7 0.2 slice_reduce_fusion
  20.0 0.3 multiply_reduce_fusion
  20.5 0.2 slice_reduce_fusion.1
  20.7 136.8 %fetch.1 = (bf16[16,12,2,64,128]{4,3,2,1,0:T(8,128)(2,1)}, bf16[2,64,2048]{2,1,0:T(8,128)(2,1)S(1)}, bf16[2,64,2048]{2,1,0:T(8,128)(2,1)S(1)}) custom-call(s32[192]{0:T(256)S(1)} %broadcast_maximum_fusion.code, bf16[256,2048]{1,0:T(8,128)(2,1)S(1)} %copy-done, bf16[256,2048]{1,0:T(8,128)(2,1)S(1)} %copy-done.1), custom_call_target="tpu_custom_call" | custom-call | bytes 300000000 | tf_op jit(solution)/shard_map/fetch/pallas_call | solution.py:101
  157.6 0.8 copy-done.5
  158.3 0.8 copy-done.7
  159.3 78.2 %all-reduce.5.cloned.1.call-done.glob = bf16[2,128,2048]{2,1,0:T(8,128)(2,1)} async-done(((bf16[2,128,2048]{2,1,0:T(8,128)(2,1)}), bf16[2,128,2048]{2,1,0:T(8,128)(2,1)}) %all-reduce.5.cloned.1.call-update) | async-done | bytes 1048592 | tf_op jit(solution)/shard_map/psum | solution.py:391
  237.6 1.2 copy-done.4
  238.8 1.0 copy-done.6
  239.8 1.0 copy-done.8
  240.9 56.8 %attend.1 = (bf16[256,2048]{1,0:T(8,128)(2,1)}, bf16[256,2048]{1,0:T(8,128)(2,1)}, f32[2,256,2048]{2,1,0:T(8,128)}, bf16[2,64,2048]{2,1,0:T(8,128)(2,1)S(1)}, bf...) custom-call(s32[2]{0:T(128)S(1)} %pad_add_fusion.place, ...), custom_call_target="tpu_custom_call" | custom-call | tf_op jit(solution)/shard_map/attend/pallas_call | solution.py:279
  297.7 0.7 copy-done.9
  298.4 0.2 copy-done.10
  298.6 143.8 %give_back.1 = (bf16[16,12,2,64,128]{4,3,2,1,0:T(8,128)(2,1)}, bf16[2,64,2048]{2,1,0:T(8,128)(2,1)}, bf16[2,64,2048]{2,1,0:T(8,128)(2,1)}) custom-call(bf16[16,12,2,64,128]{4,3,2,1,0:T(8,128)(2,1)} %get-tuple-element.25.back, bf16[2,64,2048]{2,1,0:T(8,128)(2,1)} %copy-done.9, bf16[2,64,2048]{2,1,0:T(8,128)(2,1)} %copy-done.10), custom_call_target="tpu_custom_call" | custom-call | bytes 300000000 | tf_op jit(solution)/shard_map/give_back/pallas_call | solution.py:160
  442.4 68.3 %all-reduce.7.cloned.1.call-done.glob = f32[2,128,2048]{2,1,0:T(8,128)} async-done(((f32[2,128,2048]{2,1,0:T(8,128)}), f32[2,128,2048]{2,1,0:T(8,128)}) %all-reduce.7.cloned.1.call-update) | async-done | bytes 2097168 | tf_op jit(solution)/shard_map/psum | solution.py:415
  510.7 1.6 copy-done.2
  512.3 1.0 copy-done.11
  513.3 1.0 copy-done.12
  514.4 14.7 %combine.1 = (bf16[256,2048]{1,0:T(8,128)(2,1)}, bf16[256,2048]{1,0:T(8,128)(2,1)}) custom-call(s32[192]{0:T(256)S(1)} %sub.42.code, s32[2]{0:T(128)S(1)} %pad_add_fusion.place, s32[2]{0:T(128)S(1)} %get-tuple-element.34.hit, f32[2,256,2048]{2,1,0:T(8,128)} %get-tuple-element.24.own, bf16[2,64,2048]{2,1,0:T(8,128)(2,1)S(1)} %copy-done.11, ...), custom_call_target="tpu_custom_call" | custom-call | tf_op jit(solution)/shard_map/combine/pallas_call | solution.py:353
  (44 shorter events, 0.9 us)
Async XLA Ops:
  7.2 230.4 %all-reduce.5.cloned.1.call-start = ((), (), s32[]{:S(2)}) async-start(), calls=%async_computation | async-start | bytes 2097152 | tf_op jit(solution)/shard_map/psum | solution.py:391
  15.7 1.9 copy-start.13
  16.4 4.3 copy-start
  16.5 4.3 copy-start.1
  17.5 220.0 %copy-start.3 = (bf16[256,2048]{1,0:T(8,128)(2,1)S(1)}, bf16[256,2048]{1,0:T(8,128)(2,1)}, u32[]{:S(2)}) copy-start(bf16[256,2048]{1,0:T(8,128)(2,1)} %q.1) | copy-start | bytes 3145732
  17.5 493.2 %all-reduce.7.cloned.1.call-start = ((), (), s32[]{:S(2)}) async-start(), calls=%async_computation.1 | async-start | bytes 4194304 | tf_op jit(solution)/shard_map/psum | solution.py:415
  157.5 0.8 copy-start.5
  158.3 0.8 copy-start.7
  237.6 1.2 copy-start.4
  238.8 1.0 copy-start.6
  239.8 1.0 copy-start.8
  297.6 0.8 copy-start.9
  297.6 1.0 copy-start.10
  510.7 1.6 copy-start.2
  512.3 1.0 copy-start.11
  513.3 1.0 copy-start.12
Sparse Core Ops, SparseCore 0:
  17.7 219.8 all-reduce.4
  297.8 212.8 all-reduce.6

commit v2 on v1

--- a/solution.py
+++ b/solution.py
@@ -14,6 +14,7 @@
 GLOBALS = 2
 RANDOM = 3
 MASKED = -1e30
+INNER = 4
 MESH = pl.DeviceIdType.MESH
 ANY = pl.BlockSpec(memory_space=pl.ANY)
 VMEM = pl.BlockSpec(memory_space=pltpu.VMEM)
@@ -45,19 +46,117 @@
     )
 
 
-def fetch_kernel(shards, capacity, code, k, v, got, before, after, tiles, staged, send, recv, rim_send, rim_recv, own):
+class Share:
+    def __init__(self, me, shards, src, out, land_a, quarter, land_b, piece, send, recv, far_send, far_recv, local):
+        self.inner, self.outer, self.runs = lax.rem(me, INNER), me // INNER, shards // INNER
+        self.src, self.out = src, out
+        self.land_a, self.quarter, self.land_b, self.piece = land_a, quarter, land_b, piece
+        self.near_sems = [(send.at[i], recv.at[i]) for i in range(2)]
+        self.far_sems = [(far_send.at[i], far_recv.at[i]) for i in range(2)]
+        self.local = pltpu.make_async_copy(piece, out.at[self.inner, self.outer], local)
+
+    def scatter_near(self, step, wait=False):
+        target = lax.rem(self.inner + step, INNER)
+        at = lax.rem(self.inner + INNER - step, INNER) if wait else self.inner
+        device = self.outer * INNER + target
+        return remote(self.src.at[target], self.land_a.at[at], self.near_sems[0], step, device)
+
+    def scatter_far(self, step, wait=False):
+        target = lax.rem(self.outer + step, self.runs)
+        at = lax.rem(self.outer + self.runs - step, self.runs) if wait else self.outer
+        device = target * INNER + self.inner
+        return remote(self.quarter.at[target], self.land_b.at[at], self.far_sems[0], step, device)
+
+    def hand_far(self, step, wait=False):
+        target = lax.rem(self.outer + step, self.runs)
+        at = lax.rem(self.outer + self.runs - step, self.runs) if wait else self.outer
+        device = target * INNER + self.inner
+        return remote(self.piece, self.out.at[self.inner, at], self.far_sems[1], step, device)
+
+    def hand_near(self, step, wait=False):
+        target = lax.rem(self.inner + step, INNER)
+        at = lax.rem(self.inner + INNER - step, INNER) if wait else self.inner
+        device = self.outer * INNER + target
+        return remote(self.out.at[self.inner], self.out.at[at], self.near_sems[1], step, device)
+
+    def start(self, copy, count):
+        def one(step, carry):
+            copy(step).start()
+            return carry
+
+        lax.fori_loop(1, count, one, 0)
+
+    def wait(self, copy, count):
+        def one(step, carry):
+            copy(step, True).wait()
+            return carry
+
+        lax.fori_loop(1, count, one, 0)
+
+    def phase(self, number):
+        f32 = jnp.float32
+        if number == 0:
+            self.start(self.scatter_near, INNER)
+        elif number == 1:
+            self.wait(self.scatter_near, INNER)
+            total = self.src[self.inner].astype(f32)
+            for step in range(1, INNER):
+                total += self.land_a[lax.rem(self.inner + step, INNER)].astype(f32)
+            self.quarter[...] = total.astype(self.quarter.dtype)
+            self.start(self.scatter_far, self.runs)
+        elif number == 2:
+            self.wait(self.scatter_far, self.runs)
+            total = lax.fori_loop(
+                1,
+                self.runs,
+                lambda step, t: t + self.land_b[lax.rem(self.outer + step, self.runs)].astype(f32),
+                self.quarter[self.outer].astype(f32),
+            )
+            self.piece[...] = total.astype(self.piece.dtype)
+            self.local.start()
+            self.start(self.hand_far, self.runs)
+        elif number == 3:
+            self.local.wait()
+            self.wait(self.hand_far, self.runs)
+            self.start(self.hand_near, INNER)
+        else:
+            self.wait(self.hand_near, INNER)
+
+
+def share_scratch(shape, kind):
+    inner, runs = shape[:2]
+    return [
+        pltpu.VMEM(shape, kind),
+        pltpu.VMEM(shape[1:], kind),
+        pltpu.VMEM(shape[1:], kind),
+        pltpu.VMEM(shape[2:], jnp.bfloat16),
+        pltpu.SemaphoreType.DMA((2, inner)),
+        pltpu.SemaphoreType.DMA((2, inner)),
+        pltpu.SemaphoreType.DMA((2, runs)),
+        pltpu.SemaphoreType.DMA((2, runs)),
+        pltpu.SemaphoreType.DMA,
+    ]
+
+
+def in_quarters(array, shards):
+    return array.reshape(INNER, shards // INNER, array.size // HEAD_DIM // shards, HEAD_DIM)
+
+
+def fetch_kernel(shards, capacity, code, k, v, glob, got, before, after, glob_out, tiles, staged, send, recv, rim_send, rim_recv, own, *shared):
     me = lax.axis_index("seq")
     up, down = lax.rem(me + 1, shards), lax.rem(me + shards - 1, shards)
     rows = k.shape[0]
     last = pl.ds(rows - BLOCK, BLOCK)
     initial = pl.ds(0, BLOCK)
+    enter(me, shards)
+    share = Share(me, shards, glob, glob_out, *shared)
+    share.phase(0)
     for which, ref in enumerate((k, v)):
         for block in range(rows // BLOCK):
             for head in range(HEADS):
                 tiles[block * HEADS + head, which] = ref[
                     block * BLOCK : (block + 1) * BLOCK, head * HEAD_DIM : (head + 1) * HEAD_DIM
                 ]
-    enter(me, shards)
     rims = []
     for which, ref in enumerate((k, v)):
         rims.append(remote(ref.at[last], before.at[which], (rim_send, rim_recv), which, up))
@@ -76,7 +175,10 @@
         remote(staged.at[target], got.at[me], (send, recv), step, target).start()
         return carry
 
-    lax.fori_loop(1, shards, give, 0)
+    for part in range(4):
+        lax.fori_loop(max(1, shards * part // 4), shards * (part + 1) // 4, give, 0)
+        if part < 3:
+            share.phase(part + 1)
     for rim in rims:
         rim.start()
     gather(me)
@@ -93,9 +195,10 @@
         return carry
 
     lax.fori_loop(1, shards, finish, 0)
-
-
-def fetch(code, keys, values, shards, capacity):
+    share.phase(4)
+
+
+def fetch(code, keys, values, glob, shards, capacity):
     kind = jnp.bfloat16
     width = keys.shape[1]
     return pl.pallas_call(
@@ -104,9 +207,10 @@
             jax.ShapeDtypeStruct((shards, capacity, 2, BLOCK, HEAD_DIM), kind),
             jax.ShapeDtypeStruct((2, BLOCK, width), kind),
             jax.ShapeDtypeStruct((2, BLOCK, width), kind),
-        ),
-        in_specs=[SMEM, VMEM, VMEM],
-        out_specs=(ANY, ANY, ANY),
+            jax.ShapeDtypeStruct(glob.shape, kind),
+        ),
+        in_specs=[SMEM, VMEM, VMEM, VMEM],
+        out_specs=(ANY, ANY, ANY, ANY),
         scratch_shapes=[
             pltpu.VMEM((keys.shape[0] // BLOCK * HEADS, 2, BLOCK, HEAD_DIM), kind),
             pltpu.VMEM((shards, capacity, 2, BLOCK, HEAD_DIM), kind),
@@ -115,19 +219,24 @@
             pltpu.SemaphoreType.DMA((4,)),
             pltpu.SemaphoreType.DMA((4,)),
             pltpu.SemaphoreType.DMA,
-        ],
+        ]
+        + share_scratch(glob.shape, kind),
         compiler_params=pltpu.CompilerParams(
             collective_id=0, has_side_effects=True, vmem_limit_bytes=VMEM_LIMIT
         ),
         cost_estimate=pl.CostEstimate(flops=0, bytes_accessed=300_000_000, transcendentals=0),
         name="fetch",
-    )(code, keys, values)
-
-
-def give_back_kernel(shards, back, lower, upper, got, above, below, send, recv, rim_send, rim_recv, own):
+    )(code, keys, values, glob)
+
+
+def give_back_kernel(
+    shards, back, lower, upper, glob, got, above, below, glob_out, send, recv, rim_send, rim_recv, own, *shared
+):
     me = lax.axis_index("seq")
     up, down = lax.rem(me + 1, shards), lax.rem(me + shards - 1, shards)
     enter(me, shards)
+    share = Share(me, shards, glob, glob_out, *shared)
+    share.phase(0)
     rims = [
         remote(lower, above, (rim_send, rim_recv), 0, down),
         remote(upper, below, (rim_send, rim_recv), 1, up),
@@ -138,7 +247,10 @@
         remote(back.at[target], got.at[me], (send, recv), step, target).start()
         return carry
 
-    lax.fori_loop(1, shards, give, 0)
+    for part in range(4):
+        lax.fori_loop(max(1, shards * part // 4), shards * (part + 1) // 4, give, 0)
+        if part < 3:
+            share.phase(part + 1)
     for rim in rims:
         rim.start()
     mine = pltpu.make_async_copy(back.at[me], got.at[me], own)
@@ -154,25 +266,29 @@
         return carry
 
     lax.fori_loop(1, shards, finish, 0)
-
-
-def give_back(back, lower, upper, shards):
+    share.phase(4)
+
+
+def give_back(back, lower, upper, glob, shards):
     return pl.pallas_call(
         functools.partial(give_back_kernel, shards),
-        out_shape=tuple(jax.ShapeDtypeStruct(a.shape, a.dtype) for a in (back, lower, upper)),
-        in_specs=[ANY, ANY, ANY],
-        out_specs=(ANY, ANY, ANY),
+        out_shape=tuple(jax.ShapeDtypeStruct(a.shape, jnp.bfloat16) for a in (back, lower, upper, glob)),
+        in_specs=[ANY, ANY, ANY, VMEM],
+        out_specs=(ANY, ANY, ANY, ANY),
         scratch_shapes=[
             pltpu.SemaphoreType.DMA((shards,)),
             pltpu.SemaphoreType.DMA((shards,)),
             pltpu.SemaphoreType.DMA((2,)),
             pltpu.SemaphoreType.DMA((2,)),
             pltpu.SemaphoreType.DMA,
-        ],
-        compiler_params=pltpu.CompilerParams(collective_id=1, has_side_effects=True),
+        ]
+        + share_scratch(glob.shape, glob.dtype),
+        compiler_params=pltpu.CompilerParams(
+            collective_id=1, has_side_effects=True, vmem_limit_bytes=VMEM_LIMIT
+        ),
         cost_estimate=pl.CostEstimate(flops=0, bytes_accessed=300_000_000, transcendentals=0),
         name="give_back",
-    )(back, lower, upper)
+    )(back, lower, upper, glob)
 
 
 def dot(a, b, dims):
@@ -205,46 +321,45 @@
     near[...] = jnp.zeros_like(near)
     k_all = jnp.concatenate([before[0], k[...], after[0]], 0)
     v_all = jnp.concatenate([before[1], v[...], after[1]], 0)
-    gk, gv = glob[0], glob[1]
-    glob_k = jnp.zeros((n_glob, HEAD_DIM), f32)
-    glob_v = jnp.zeros((n_glob, HEAD_DIM), f32)
-    for j in range(blocks):
-        rows = pl.ds(j * BLOCK, BLOCK)
-        span = slice(j * BLOCK, j * BLOCK + n_near)
-        qj, dj = q[rows, :], d[rows, :]
-        picked = [rand[j * RANDOM + r] for r in range(RANDOM)]
-        kj = jnp.concatenate([k_all[span], gk] + [x[0, 0, 0] for x in picked], 0)
-        vj = jnp.concatenate([v_all[span], gv] + [x[0, 0, 1] for x in picked], 0)
-        s = dot(qj, kj, ((1,), (1,))) * scale
-        if j == 0 or j == blocks - 1:
-            column = lax.broadcasted_iota(jnp.int32, s.shape, 1)
-            if j == 0:
-                s = jnp.where((column < BLOCK) & (place[0] == 0), MASKED, s)
-            if j == blocks - 1:
-                outside = (column >= 2 * BLOCK) & (column < n_near) & (place[1] == 0)
-                s = jnp.where(outside, MASKED, s)
-        e = jnp.exp(s - jnp.max(s, -1, keepdims=True))
-        p = e * (1.0 / jnp.sum(e, -1, keepdims=True))
-        pb = p.astype(b16)
-        attended[rows, :] = dot(pb, vj, ((1,), (0,))).astype(b16)
-        gp = dot(dj, vj, ((1,), (1,)))
-        delta = jnp.sum(p * gp, -1, keepdims=True)
-        ds = (p * (gp - delta)).astype(b16)
-        grad_q[rows, :] = (scale * dot(ds, kj, ((1,), (0,)))).astype(b16)
-        dk = scale * dot(ds, qj, ((0,), (0,)))
-        dv = dot(pb, dj, ((0,), (0,)))
-        near[0, span] += dk[:n_near]
-        near[1, span] += dv[:n_near]
-        glob_k += dk[n_near : n_near + n_glob]
-        glob_v += dv[n_near : n_near + n_glob]
+    gk, gv = glob[0, 0], glob[0, 1]
+    each = range(blocks)
+    rows = [slice(j * BLOCK, (j + 1) * BLOCK) for j in each]
+    span = [slice(j * BLOCK, j * BLOCK + n_near) for j in each]
+    picked = [[rand[j * RANDOM + r] for r in range(RANDOM)] for j in each]
+    qs = [q[rows[j], :] for j in each]
+    gs = [d[rows[j], :] for j in each]
+    ks = [jnp.concatenate([k_all[span[j]], gk] + [x[0, 0, 0] for x in picked[j]], 0) for j in each]
+    vs = [jnp.concatenate([v_all[span[j]], gv] + [x[0, 0, 1] for x in picked[j]], 0) for j in each]
+    scores = [dot(qs[j], ks[j], ((1,), (1,))) * scale for j in each]
+    gps = [dot(gs[j], vs[j], ((1,), (1,))) for j in each]
+    column = lax.broadcasted_iota(jnp.int32, scores[0].shape, 1)
+    scores[0] = jnp.where((column < BLOCK) & (place[0] == 0), MASKED, scores[0])
+    outside = (column >= 2 * BLOCK) & (column < n_near) & (place[1] == 0)
+    scores[-1] = jnp.where(outside, MASKED, scores[-1])
+    es = [jnp.exp(x - jnp.max(x, -1, keepdims=True)) for x in scores]
+    ps = [x * (1.0 / jnp.sum(x, -1, keepdims=True)) for x in es]
+    pbs = [x.astype(b16) for x in ps]
+    deltas = [jnp.sum(ps[j] * gps[j], -1, keepdims=True) for j in each]
+    dss = [(ps[j] * (gps[j] - deltas[j])).astype(b16) for j in each]
+    dks = [scale * dot(dss[j], qs[j], ((0,), (0,))) for j in each]
+    dvs = [dot(pbs[j], gs[j], ((0,), (0,))) for j in each]
+    outs = [dot(pbs[j], vs[j], ((1,), (0,))).astype(b16) for j in each]
+    gqs = [(scale * dot(dss[j], ks[j], ((1,), (0,)))).astype(b16) for j in each]
+    for j in each:
         for r in range(RANDOM):
             item = j * RANDOM + r
             at = slice(n_near + n_glob + r * BLOCK, n_near + n_glob + (r + 1) * BLOCK)
-            terms[slot, item, 0] = dk[at].astype(b16)
-            terms[slot, item, 1] = dv[at].astype(b16)
-            out_copy(head, slot, item).start()
-    glob_grad[0] = glob_k
-    glob_grad[1] = glob_v
+            terms[slot, item, 0] = dks[j][at].astype(b16)
+            terms[slot, item, 1] = dvs[j][at].astype(b16)
+    for item in range(items):
+        out_copy(head, slot, item).start()
+    for j in each:
+        attended[rows[j], :] = outs[j]
+        grad_q[rows[j], :] = gqs[j]
+        near[0, span[j]] += dks[j][:n_near]
+        near[1, span[j]] += dvs[j][:n_near]
+    glob_grad[0, 0] = sum(x[n_near : n_near + n_glob] for x in dks)
+    glob_grad[0, 1] = sum(x[n_near : n_near + n_glob] for x in dvs)
     own_grad[...] = near[:, BLOCK : (blocks + 1) * BLOCK]
     lower[...] = near[:, :BLOCK].astype(b16)
     upper[...] = near[:, (blocks + 1) * BLOCK :].astype(b16)
@@ -276,14 +391,15 @@
         return pl.BlockSpec((1, 1, 2, BLOCK, HEAD_DIM), at)
 
     n_glob = GLOBALS * BLOCK
+    shared = pl.BlockSpec((1, 2, n_glob, HEAD_DIM), lambda h, *_: (h, 0, 0, 0))
     return pl.pallas_call(
         functools.partial(attend_kernel, blocks),
         grid_spec=pltpu.PrefetchScalarGridSpec(
             num_scalar_prefetch=3,
             grid=(HEADS,),
-            in_specs=[flat(), flat(), flat(), flat(), pair(BLOCK), pair(BLOCK), pair(n_glob)]
+            in_specs=[flat(), flat(), flat(), flat(), pair(BLOCK), pair(BLOCK), shared]
             + [picked(item) for item in range(items)],
-            out_specs=[flat(), flat(), pair(rows), pair(BLOCK), pair(BLOCK), pair(n_glob), ANY],
+            out_specs=[flat(), flat(), pair(rows), pair(BLOCK), pair(BLOCK), shared, ANY],
             scratch_shapes=[
                 pltpu.VMEM((2, rows + 2 * BLOCK, HEAD_DIM), f32),
                 pltpu.VMEM((2, items, 2, BLOCK, HEAD_DIM), b16),
@@ -296,7 +412,7 @@
             jax.ShapeDtypeStruct((2, rows, width), f32),
             jax.ShapeDtypeStruct((2, BLOCK, width), b16),
             jax.ShapeDtypeStruct((2, BLOCK, width), b16),
-            jax.ShapeDtypeStruct((2, n_glob, width), f32),
+            jax.ShapeDtypeStruct(glob.shape, f32),
             jax.ShapeDtypeStruct(got.shape, b16),
         ),
         compiler_params=pltpu.CompilerParams(vmem_limit_bytes=VMEM_LIMIT),
@@ -325,7 +441,9 @@
             @pl.when(hit[g] >= 0)
             def _():
                 at = pl.ds(pl.multiple_of(hit[g] * BLOCK, BLOCK), BLOCK)
-                acc[:, at] += glob[:, g * BLOCK : (g + 1) * BLOCK]
+                for head in range(HEADS):
+                    column = slice(head * HEAD_DIM, (head + 1) * HEAD_DIM)
+                    acc[:, at, column] += glob[head, :, g * BLOCK : (g + 1) * BLOCK].astype(jnp.float32)
 
     for slot in range(capacity):
         packed = code[source * capacity + slot]
@@ -347,7 +465,7 @@
     rows, width = own.shape[1:]
 
     def whole(a):
-        return pl.BlockSpec(a.shape, lambda s, *_: (0, 0, 0))
+        return pl.BlockSpec(a.shape, lambda s, *_: (0,) * a.ndim)
 
     out = pl.BlockSpec((rows, width), lambda s, *_: (0, 0))
     return pl.pallas_call(
@@ -388,7 +506,8 @@
             [lax.dynamic_slice_in_dim(a, start, BLOCK, 0) for a in (keys, values)], 0
         )
         parts.append(jnp.where(mine[g], pair, jnp.zeros_like(pair)))
-    glob = lax.psum(jnp.concatenate(parts, 1), "seq")
+    glob = jnp.concatenate(parts, 1).reshape(2, GLOBALS * BLOCK, HEADS, HEAD_DIM)
+    glob = jnp.transpose(glob, (2, 0, 1, 3))
 
     wanted = lax.dynamic_slice_in_dim(random_blocks, me * blocks, blocks, 1).reshape(-1)
     requests = wanted.shape[0]
@@ -407,13 +526,18 @@
     entry = asked % blocks * HEADS + item_head[None, :] + 1
     code = (jnp.sum(chosen * entry[:, :, None], 1) - 1).reshape(-1)
 
-    got, before, after = fetch(jnp.maximum(code, 0), keys, values, shards, capacity)
+    got, before, after, glob_all = fetch(
+        jnp.maximum(code, 0), keys, values, in_quarters(glob, shards), shards, capacity
+    )
+    glob = glob_all.reshape(glob.shape)
     place = jnp.stack([me, shards - 1 - me]).astype(i32)
     attended, grad_q, own_grad, lower, upper, glob_grad, back = attend(
         place, owner, rank, queries, grad_out, keys, values, before, after, glob, got
     )
-    glob_sum = lax.psum(glob_grad, "seq")
-    returned, above, below = give_back(back, lower, upper, shards)
+    returned, above, below, glob_sum = give_back(
+        back, lower, upper, in_quarters(glob_grad, shards), shards
+    )
+    glob_sum = glob_sum.reshape(glob.shape)
     hit = jnp.where(mine, global_blocks % blocks, -1).astype(i32)
     grad_k, grad_v = combine(code, place, hit, own_grad, above, below, glob_sum, returned)
     return attended, grad_q, grad_k, grad_v

time: 541 us -> 451 us (0.83)
  waiting for transfers between devices: 147 us -> 0 us
  Pallas kernels: 352 us -> 433 us
  between operations: 18.2 us -> 4.82 us
    psum x2 -> x0, waiting for transfers between devices: 147 us -> none  [the longest x1 78.2 us: on_device(): glob = lax.psum(jnp.concatenate(parts, 1), 'seq')]
    pallas_call x1, Pallas kernels: 144 us -> 202 us  [give_back(): pl.pallas_call(functools.partial(give_back_kernel, shards), out_shape=tup...]
    pallas_call x1, Pallas kernels: 137 us -> 186 us  [fetch(): pl.pallas_call(functools.partial(fetch_kernel, shards, capacity), out_sha...]
    pallas_call x1, Pallas kernels: 56.8 us -> 30 us  [attend(): pl.pallas_call(functools.partial(attend_kernel, blocks), grid_spec=pltpu....]
  transfers between devices with their start and end apart: 2 -> 0, of which waited for: 2 -> 0; matrix products, arithmetic and copies ran while one was open for 1% -> 0% of each run, Pallas kernels for 52% -> 0%
where the time goes in v2:
time: 451 us
  Pallas kernels  433 us (96%)
  local copies, waits for them, and re-layouts  9.07 us (2%)
  between operations  4.82 us (1%)
    pallas_call x1, Pallas kernels, give_back(): pl.pallas_call(functools.partial(give_back_kernel, shards), out_shape=tup...  202 us
    pallas_call x1, Pallas kernels, fetch(): pl.pallas_call(functools.partial(fetch_kernel, shards, capacity), out_sha...  186 us
    pallas_call x1, Pallas kernels, attend(): pl.pallas_call(functools.partial(attend_kernel, blocks), grid_spec=pltpu....  30 us
    pallas_call x1, Pallas kernels, combine(): pl.pallas_call(functools.partial(combine_kernel, capacity, rows // BLOCK)...  14.9 us

profile of v2, /device:TPU:25, one launch (start us, length us, event | category | flops | bytes accessed | tf_op | source)
XLA Modules:
  0.0 450.8 jit_solution(11981861382343540365)
XLA Ops:
  0.6 0.0 copy-start
  0.7 0.9 fusion.9
  1.5 0.7 fusion.12
  2.2 1.3 fusion.13
  7.4 0.8 constant_dynamic-slice_fusion
  8.2 0.2 copy.50
  8.5 0.1 reshape.173
  8.6 0.6 reduce-window.14
  9.2 0.2 slice_reduce_fusion.1
  9.5 0.1 bitcast_bitcast_fusion
  9.6 0.8 copy.53
  10.4 0.1 copy.54
  10.6 0.1 copy.55
  10.7 0.6 reduce-window.16
  11.3 0.2 slice_reduce_fusion
  11.6 0.1 copy_bitcast_fusion
  11.7 0.3 multiply_reduce_fusion
  12.0 0.1 copy.61
  12.0 0.1 sub.42.code
  12.1 1.3 dynamic-slice_bitcast_fusion.2
  13.5 0.0 copy-start.3
  13.5 0.0 copy-start.4
  13.6 0.9 maximum_select_fusion.1
  14.5 0.7 maximum_select_fusion
  15.2 0.1 maximum_bitcast_fusion
  15.3 0.3 copy.62
  15.6 186.1 %fetch.1 = (bf16[16,12,2,64,128]{4,3,2,1,0:T(8,128)(2,1)}, bf16[2,64,2048]{2,1,0:T(8,128)(2,1)S(1)}, bf16[2,64,2048]{2,1,0:T(8,128)(2,1)S(1)}, bf16[4,4,256,128]{3,2,1,0:T(8,128)(2,1)S(1)}) custom-call(s32[192]{0:T(256)S(1)} %broadcast_maximum_fusion.code, bf16[256,2048]{1,0:T(8,128)(2,1)S(1)} %copy-done, bf16[256,2048]{1,0:T(8,128)(2,1)S(1)} %copy-done.1, ...), custom_call_target="tpu_custom_call" | custom-call | bytes 300000000 | tf_op jit(solution)/shard_map/fetch/pallas_call | solution.py:204
  201.8 1.0 copy-done.5
  202.8 30.0 %attend.1 = (bf16[256,2048]{1,0:T(8,128)(2,1)}, bf16[256,2048]{1,0:T(8,128)(2,1)}, f32[2,256,2048]{2,1,0:T(8,128)}, bf16[2,64,2048]{2,1,0:T(8,128)(2,1)S(1)}, bf...) custom-call(s32[2]{0:T(128)S(1)} %get-tuple-element.50.place, ...), custom_call_target="tpu_custom_call" | custom-call | tf_op jit(solution)/shard_map/attend/pallas_call | solution.py:395
  232.7 1.6 copy-done.2
  234.3 201.6 %give_back.1 = (bf16[16,12,2,64,128]{4,3,2,1,0:T(8,128)(2,1)}, bf16[2,64,2048]{2,1,0:T(8,128)(2,1)S(1)}, bf16[2,64,2048]{2,1,0:T(8,128)(2,1)S(1)}, bf16[4,4,256,128]{3,2,1,0:T(8,128)(2,1)S(1)}) custom-call(bf16[16,12,2,64,128]{4,3,2,1,0:T(8,128)(2,1)} %get-tuple-element.28.back, bf16[2,64,2048]{2,1,0:T(8,128)(2,1)S(1)} %get-tuple-element.29.lower, ...), custom_call_target="tpu_custom_call" | custom-call | bytes 300000000 | tf_op jit(solution)/shard_map/give_back/pallas_call | solution.py:273
  435.9 14.9 %combine.1 = (bf16[256,2048]{1,0:T(8,128)(2,1)}, bf16[256,2048]{1,0:T(8,128)(2,1)}) custom-call(s32[192]{0:T(256)S(1)} %sub.42.code, s32[2]{0:T(128)S(1)} %get-tuple-element.50.place, s32[2]{0:T(128)S(1)} %get-tuple-element.38.hit, f32[2,256,2048]{2,1,0:T(8,128)} %get-tuple-element.27.own, bf16[2,64,2048]{2,1,0:T(8,128)(2,1)S(1)} %get-tuple-element.32.above, ...), custom_call_target="tpu_custom_call" | custom-call | tf_op jit(solution)/shard_map/combine/pallas_call | solution.py:471
  (26 shorter events, 0.4 us)
Async XLA Ops:
  0.6 15.0 %copy-start.1 = (bf16[256,2048]{1,0:T(8,128)(2,1)S(1)}, bf16[256,2048]{1,0:T(8,128)(2,1)}, u32[]{:S(2)}) copy-start(bf16[256,2048]{1,0:T(8,128)(2,1)} %v.3) | copy-start | bytes 3145732
  0.6 15.0 %copy-start = (bf16[256,2048]{1,0:T(8,128)(2,1)S(1)}, bf16[256,2048]{1,0:T(8,128)(2,1)}, u32[]{:S(2)}) copy-start(bf16[256,2048]{1,0:T(8,128)(2,1)} %k.3) | copy-start | bytes 3145732
  13.5 189.3 %copy-start.3 = (bf16[256,2048]{1,0:T(8,128)(2,1)S(1)}, bf16[256,2048]{1,0:T(8,128)(2,1)}, u32[]{:S(2)}) copy-start(bf16[256,2048]{1,0:T(8,128)(2,1)} %q.1) | copy-start | bytes 3145732
  13.5 189.3 %copy-start.4 = (bf16[256,2048]{1,0:T(8,128)(2,1)S(1)}, bf16[256,2048]{1,0:T(8,128)(2,1)}, u32[]{:S(2)}) copy-start(bf16[256,2048]{1,0:T(8,128)(2,1)} %d.1) | copy-start | bytes 3145732
  201.8 1.0 copy-start.5
  232.7 1.6 copy-start.2

commit v3 on v2

--- a/solution.py
+++ b/solution.py
@@ -170,13 +170,14 @@
         lax.fori_loop(0, capacity, item, 0)
 
     def give(step, carry):
+        step = lax.rem(step * (shards // 2 - 1), shards)
         target = lax.rem(me + step, shards)
         gather(target)
         remote(staged.at[target], got.at[me], (send, recv), step, target).start()
         return carry
 
-    for part in range(4):
-        lax.fori_loop(max(1, shards * part // 4), shards * (part + 1) // 4, give, 0)
+    for part in range(8):
+        lax.fori_loop(max(1, shards * part // 8), shards * (part + 1) // 8, give, 0)
         if part < 3:
             share.phase(part + 1)
     for rim in rims:
@@ -189,6 +190,7 @@
         rim.wait()
 
     def finish(step, carry):
+        step = lax.rem(step * (shards // 2 - 1), shards)
         target = lax.rem(me + step, shards)
         source = lax.rem(me + shards - step, shards)
         remote(staged.at[target], got.at[source], (send, recv), step, target).wait()
@@ -243,6 +245,7 @@
     ]
 
     def give(step, carry):
+        step = lax.rem(step * (shards // 2 - 1), shards)
         target = lax.rem(me + step, shards)
         remote(back.at[target], got.at[me], (send, recv), step, target).start()
         return carry
@@ -260,6 +263,7 @@
         rim.wait()
 
     def finish(step, carry):
+        step = lax.rem(step * (shards // 2 - 1), shards)
         target = lax.rem(me + step, shards)
         source = lax.rem(me + shards - step, shards)
         remote(back.at[target], got.at[source], (send, recv), step, target).wait()
@@ -535,7 +539,7 @@
         place, owner, rank, queries, grad_out, keys, values, before, after, glob, got
     )
     returned, above, below, glob_sum = give_back(
-        back, lower, upper, in_quarters(glob_grad, shards), shards
+        back, lower, upper, in_quarters(glob_grad.astype(jnp.bfloat16), shards), shards
     )
     glob_sum = glob_sum.reshape(glob.shape)
     hit = jnp.where(mine, global_blocks % blocks, -1).astype(i32)

time: 451 us -> 384 us (0.85)
  Pallas kernels: 433 us -> 364 us
    pallas_call x1, Pallas kernels: 202 us -> 158 us  [give_back(): pl.pallas_call(functools.partial(give_back_kernel, shards), out_shape=tup...]
    pallas_call x1, Pallas kernels: 186 us -> 162 us  [fetch(): pl.pallas_call(functools.partial(fetch_kernel, shards, capacity), out_sha...]
where the time goes in v3:
time: 384 us; the launch traced here: 383 us
  Pallas kernels  364 us (95%)
  local copies, waits for them, and re-layouts  7.48 us (2%)
  other arithmetic  6.1 us (2%)
  between operations  4.82 us (1%)
    pallas_call x1, Pallas kernels, fetch(): pl.pallas_call(functools.partial(fetch_kernel, shards, capacity), out_sha...  162 us
    pallas_call x1, Pallas kernels, give_back(): pl.pallas_call(functools.partial(give_back_kernel, shards), out_shape=tup...  158 us
    pallas_call x1, Pallas kernels, attend(): pl.pallas_call(functools.partial(attend_kernel, blocks), grid_spec=pltpu....  30 us
    pallas_call x1, Pallas kernels, combine(): pl.pallas_call(functools.partial(combine_kernel, capacity, rows // BLOCK)...  14.9 us

profile of v3, /device:TPU:25, one launch (start us, length us, event | category | flops | bytes accessed | tf_op | source)
XLA Modules:
  0.0 382.8 jit_solution(5610359125544767366)
XLA Ops:
  0.6 0.0 copy-start.1
  0.7 0.9 fusion.9
  1.5 0.7 fusion.12
  2.2 1.3 fusion.13
  7.4 0.8 constant_dynamic-slice_fusion
  8.2 0.2 copy.50
  8.5 0.1 reshape.173
  8.6 0.6 reduce-window.14
  9.2 0.2 slice_reduce_fusion.1
  9.5 0.1 bitcast_bitcast_fusion
  9.6 0.8 copy.53
  10.4 0.1 copy.54
  10.6 0.1 copy.55
  10.7 0.6 reduce-window.16
  11.3 0.2 slice_reduce_fusion
  11.6 0.1 copy_bitcast_fusion
  11.7 0.3 multiply_reduce_fusion
  12.0 0.1 copy.61
  12.0 0.1 sub.42.code
  12.1 1.3 dynamic-slice_bitcast_fusion.2
  13.5 0.0 copy-start.3
  13.6 0.9 maximum_select_fusion.1
  14.5 0.7 maximum_select_fusion
  15.2 0.1 maximum_bitcast_fusion
  15.3 0.3 copy.62
  15.6 162.0 %fetch.1 = (bf16[16,12,2,64,128]{4,3,2,1,0:T(8,128)(2,1)}, bf16[2,64,2048]{2,1,0:T(8,128)(2,1)S(1)}, bf16[2,64,2048]{2,1,0:T(8,128)(2,1)S(1)}, bf16[4,4,256,128]{3,2,1,0:T(8,128)(2,1)S(1)}) custom-call(s32[192]{0:T(256)S(1)} %broadcast_maximum_fusion.code, bf16[256,2048]{1,0:T(8,128)(2,1)S(1)} %copy-done, bf16[256,2048]{1,0:T(8,128)(2,1)S(1)} %copy-done.1, ...), custom_call_target="tpu_custom_call" | custom-call | bytes 300000000 | tf_op jit(solution)/shard_map/fetch/pallas_call | solution.py:206
  177.7 0.0 copy-start.4
  177.7 1.0 copy-done.4
  178.7 30.0 %attend.1 = (bf16[256,2048]{1,0:T(8,128)(2,1)}, bf16[256,2048]{1,0:T(8,128)(2,1)}, f32[2,256,2048]{2,1,0:T(8,128)}, bf16[2,64,2048]{2,1,0:T(8,128)(2,1)S(1)}, bf...) custom-call(s32[2]{0:T(128)S(1)} %get-tuple-element.50.place, ...), custom_call_target="tpu_custom_call" | custom-call | tf_op jit(solution)/shard_map/attend/pallas_call | solution.py:399
  208.6 1.7 convert_element_type.17
  210.4 157.5 %give_back.1 = (bf16[16,12,2,64,128]{4,3,2,1,0:T(8,128)(2,1)}, bf16[2,64,2048]{2,1,0:T(8,128)(2,1)S(1)}, bf16[2,64,2048]{2,1,0:T(8,128)(2,1)S(1)}, bf16[4,4,256,128]{3,2,1,0:T(8,128)(2,1)S(1)}) custom-call(bf16[16,12,2,64,128]{4,3,2,1,0:T(8,128)(2,1)} %get-tuple-element.28.back, bf16[2,64,2048]{2,1,0:T(8,128)(2,1)S(1)} %get-tuple-element.29.lower, ...), custom_call_target="tpu_custom_call" | custom-call | bytes 300000000 | tf_op jit(solution)/shard_map/give_back/pallas_call | solution.py:277
  367.9 14.9 %combine.1 = (bf16[256,2048]{1,0:T(8,128)(2,1)}, bf16[256,2048]{1,0:T(8,128)(2,1)}) custom-call(s32[192]{0:T(256)S(1)} %sub.42.code, s32[2]{0:T(128)S(1)} %get-tuple-element.50.place, s32[2]{0:T(128)S(1)} %get-tuple-element.38.hit, f32[2,256,2048]{2,1,0:T(8,128)} %get-tuple-element.27.own, bf16[2,64,2048]{2,1,0:T(8,128)(2,1)S(1)} %get-tuple-element.32.above, ...), custom_call_target="tpu_custom_call" | custom-call | tf_op jit(solution)/shard_map/combine/pallas_call | solution.py:475
  (25 shorter events, 0.4 us)
Async XLA Ops:
  0.6 15.0 %copy-start.1 = (bf16[256,2048]{1,0:T(8,128)(2,1)S(1)}, bf16[256,2048]{1,0:T(8,128)(2,1)}, u32[]{:S(2)}) copy-start(bf16[256,2048]{1,0:T(8,128)(2,1)} %v.3) | copy-start | bytes 3145732
  0.6 15.0 %copy-start = (bf16[256,2048]{1,0:T(8,128)(2,1)S(1)}, bf16[256,2048]{1,0:T(8,128)(2,1)}, u32[]{:S(2)}) copy-start(bf16[256,2048]{1,0:T(8,128)(2,1)} %k.3) | copy-start | bytes 3145732
  13.5 165.2 %copy-start.2 = (bf16[256,2048]{1,0:T(8,128)(2,1)S(1)}, bf16[256,2048]{1,0:T(8,128)(2,1)}, u32[]{:S(2)}) copy-start(bf16[256,2048]{1,0:T(8,128)(2,1)} %q.1) | copy-start | bytes 3145732
  13.5 165.2 %copy-start.3 = (bf16[256,2048]{1,0:T(8,128)(2,1)S(1)}, bf16[256,2048]{1,0:T(8,128)(2,1)}, u32[]{:S(2)}) copy-start(bf16[256,2048]{1,0:T(8,128)(2,1)} %d.1) | copy-start | bytes 3145732
  177.7 1.0 copy-start.4
